TPU v7x, 32 devices: a whole 2x2x4 slice. The times are simulated.
32 devices in a mesh: groups: 2 (over x), dp: 16 (over z, y, core).
Axes of the slice: x: 2, y: 2, z: 4, core: 2. Of those that a mesh axis runs over, the one named last changes fastest.
Arguments:
- tokens: bfloat16 [8192, 8192], P(('groups', 'dp')), parts along dimension 0, may hold values from -6 to 6
- chosen_rows: bfloat16 [8192, 8192], P(('groups', 'dp')), parts along dimension 0, may hold values from -0.0625 to 0.0625
- adapter_down: bfloat16 [8192, 256], P('dp'), may hold values from -0.0625 to 0.0625
- adapter_up: bfloat16 [256, 8192], P(None, 'dp'), may hold values from -0.375 to 0.375
- lengths: int32 [32], P(('groups', 'dp')), parts along dimension 0, may hold values from 1 to 256
- parent: int32 [32], P(('groups', 'dp')), parts along dimension 0, may hold values from 0 to 7
- depth: int32 [32], P(('groups', 'dp')), parts along dimension 0, may hold values from 0 to 7
- reward: float32 [32], P(('groups', 'dp')), parts along dimension 0, may hold values from -6 to 6
Outputs:
- grad_down: float32 [16384, 256], P(('groups', 'dp')), parts along dimension 0
- grad_up: float32 [512, 8192], P('groups', 'dp'), parts along dimension 0
- advantage: float32 [32, 256], P(('groups', 'dp')), parts along dimension 0
There are 2 independent parts, one for each index of `groups`. A program takes and returns all parts, laid end to end along the dimension named above; an argument that names none is the same for every part. Nothing has to cross between parts.
All inputs are finite; a program needn't handle non-finite values.
Results may differ from a plain program's by a relative error of at most 0.0043.
Values may be sent and summed in bfloat16 or wider, within the bound.
A program may use at most 128 MiB of HBM per device.

v0:
```python
import jax
import jax.numpy as jnp
from jax import lax
from jax.sharding import PartitionSpec as P

SEG_LEN = 256
DEPTHS = 8


def body(tokens, chosen_rows, adapter_down, adapter_up, lengths, parent, depth, reward):
    parts = lax.axis_size("dp")
    seg_local = lengths.shape[0]
    segs_all = seg_local * parts
    high = lax.Precision.HIGHEST
    down_full, up_full = (
        lax.all_gather(adapter_down, "dp", axis=0, tiled=True),
        lax.all_gather(adapter_up, "dp", axis=1, tiled=True),
    )
    latent = jnp.dot(tokens, down_full, preferred_element_type=jnp.float32).astype(jnp.bfloat16)
    mixed = tokens.astype(jnp.float32) + jnp.dot(
        latent, up_full, preferred_element_type=jnp.float32
    )
    score = jnp.sum(mixed * chosen_rows.astype(jnp.float32), axis=1).reshape(seg_local, SEG_LEN)
    position = lax.broadcasted_iota(jnp.int32, (seg_local, SEG_LEN), 1)
    valid = (position < lengths[:, None]).astype(jnp.float32)
    masked = score * valid
    parent_hot = (parent[None, :] == jnp.arange(segs_all, dtype=jnp.int32)[:, None]).astype(
        jnp.float32
    )
    depth_hot = (depth[None, :] == jnp.arange(DEPTHS, dtype=jnp.int32)[:, None]).astype(jnp.float32)
    group_part = jnp.dot(parent_hot, masked, precision=high)
    group_tally = jnp.sum(parent_hot, axis=1)
    depth_part = jnp.dot(depth_hot, masked, precision=high)
    depth_tally = jnp.sum(depth_hot, axis=1)
    group_sum, group_count, depth_sum, depth_count = lax.psum(
        (group_part, group_tally, depth_part, depth_tally), "dp"
    )
    sibling_mean = group_sum / jnp.maximum(group_count, 1.0)[:, None]
    depth_mean = depth_sum / jnp.maximum(depth_count, 1.0)[:, None]
    own_sibling = jnp.dot(parent_hot.T, sibling_mean, precision=high)
    own_depth = jnp.dot(depth_hot.T, depth_mean, precision=high)
    advantage = (reward[:, None] + masked - own_sibling - 0.5 * own_depth) * valid
    weight = -advantage.reshape(-1)
    slope = (weight[:, None] * chosen_rows.astype(jnp.float32)).astype(jnp.bfloat16)
    latent_grad = lax.dot_general(
        slope, up_full, (((1,), (1,)), ((), ())), preferred_element_type=jnp.float32
    ).astype(jnp.bfloat16)
    scale = 1.0 / jnp.sqrt(jnp.float32(tokens.shape[0] * parts))
    up_term = lax.dot_general(
        latent, slope, (((0,), (0,)), ((), ())), preferred_element_type=jnp.float32
    )
    grad_up = lax.psum_scatter(up_term, "dp", scatter_dimension=1, tiled=True) * scale
    grad_down = (
        lax.psum_scatter(
            lax.dot_general(
                tokens, latent_grad, (((0,), (0,)), ((), ())), preferred_element_type=jnp.float32
            ),
            "dp",
            scatter_dimension=0,
            tiled=True,
        )
        * scale
    )
    return (grad_down, grad_up, advantage)


def solution(mesh):
    in_specs = (
        P(("groups", "dp"), None),
        P(("groups", "dp"), None),
        P("dp", None),
        P(None, "dp"),
        P(("groups", "dp")),
        P(("groups", "dp")),
        P(("groups", "dp")),
        P(("groups", "dp")),
    )
    out_specs = (P(("groups", "dp"), None), P("groups", "dp"), P(("groups", "dp"), None))
    return jax.shard_map(body, mesh=mesh, in_specs=in_specs, out_specs=out_specs, check_vma=False)
```

profile of v0, /device:TPU:0, one launch (start us, length us, event | category | flops | bytes accessed | tf_op | source)
XLA Modules:
  0.0 415.7 jit_solution(6731779702622472773)
XLA Ops:
  7.2 0.0 all-gather.3.cloned.1.call-start
  7.2 0.7 all-gather.3.cloned.1.call-update
  7.9 0.0 all-gather.5.cloned.1.call-start
  7.9 0.7 all-gather.5.cloned.1.call-update
  8.6 0.0 reduce-scatter.3.cloned.1.call-start
  11.3 52.1 %all-gather.3.cloned.1.call-done = bf16[8192,256]{1,0:T(8,128)(2,1)} async-done(((bf16[512,256]{1,0:T(8,128)(2,1)}), bf16[8192,256]{1,0:T(8,128)(2,1)}) %all-gather.3.cloned.1.call-update) | async-done | bytes 4194320 | tf_op jit(solution)/shard_map/all_gather | solution.py:16
  63.5 4.7 %convolution_convert_fusion = bf16[256,256]{1,0:T(8,128)(2,1)S(1)} fusion(bf16[256,8192]{1,0:T(8,128)(2,1)} %param.8, bf16[8192,256]{1,0:T(8,128)(2,1)} %all-gather.3.cloned.1.call-done), kind=kOutput, calls=%fused_computation.9 | convolution fusion | flops 1073807360 | bytes 8519680 | tf_op jit(solution)/shard_map/dot_general | solution.py:19
  68.2 49.2 %all-gather.5.cloned.1.call-done = bf16[256,8192]{1,0:T(8,128)(2,1)} async-done(((bf16[256,512]{1,0:T(8,128)(2,1)}), bf16[256,8192]{1,0:T(8,128)(2,1)}) %all-gather.5.cloned.1.call-update) | async-done | bytes 4194320 | tf_op jit(solution)/shard_map/all_gather | solution.py:17
  117.3 6.7 %fusion.2 = f32[256]{0:T(256)S(1)} fusion(bf16[256,8192]{1,0:T(8,128)(2,1)} %param.9, bf16[256,256]{1,0:T(8,128)(2,1)S(1)} %convolution_convert_fusion, bf16[256,8192]{1,0:T(8,128)(2,1)} %all-gather.5.cloned.1.call-done, bf16[256,8192]{1,0:T(8,128)(2,1)} %param.8), kind=kOutput, calls=%fused_computation.5 | convolution fusion | flops 1084227328 | bytes 12715008 | tf_op jit(solution)/shard_map/dot_general | solution.py:20
  124.1 0.1 broadcast_multiply_fusion.3
  124.1 0.1 broadcast_multiply_fusion.2
  124.2 58.9 %all-reduce = (f32[8,256]{1,0:T(8,128)S(1)}, f32[8]{0:T(128)S(1)}, f32[16,256]{1,0:T(8,128)S(1)}, f32[16]{0:T(128)S(1)}) all-reduce(f32[8,256]{1,0:T(8,128)S(1)} %broadcast_multiply_fusion.3, f32[8]{0:T(128)S(1)} %compare_convert_fusion.2, f32[16,256]{1,0:T(8,128)S(1)} %broadcast_multiply_fusion.2, ...), channel_id=1, replica_groups=mesh['groups'=2,'dp'=16] {'dp'}, use_global_device_ids=true, to_apply=%region_3.0 | all-reduce | flops 6168 | bytes 49344 | tf_op jit(solution)/shard_map/psum | solution.py:35
  183.1 0.2 fusion.13
  183.3 0.2 fusion.10
  183.5 0.6 fusion.26
  184.1 12.6 %convolution_bitcast_fusion = f32[8192,256]{0,1:T(8,128)} fusion(bf16[256,8192]{1,0:T(8,128)(2,1)} %param.8, bf16[256,8192]{1,0:T(8,128)(2,1)} %all-gather.5.cloned.1.call-done, bf16[256,8192]{1,0:T(8,128)(2,1)} %param.9, f32[256]{0:T(256)S(1)} %get-tuple-element.10), kind=kOutput, calls=%fused_computation | convolution fusion | flops 2153840640 | bytes 20972544 | tf_op jit(solution)/shard_map/dot_general | solution.py:55
  196.7 0.0 reduce-scatter.3.cloned.1.call-update
  196.7 0.0 reduce-scatter.5.cloned.1.call-start
  196.7 7.3 %fusion.3 = f32[256,8192]{1,0:T(8,128)} fusion(bf16[256,256]{1,0:T(8,128)(2,1)S(1)} %convolution_convert_fusion, bf16[256,8192]{1,0:T(8,128)(2,1)} %param.9, f32[256]{0:T(256)S(1)} %get-tuple-element.10), kind=kOutput, calls=%fused_computation.6 | convolution fusion | flops 1080033280 | bytes 12715008 | tf_op jit(solution)/shard_map/dot_general | solution.py:49
  204.0 0.0 reduce-scatter.5.cloned.1.call-update
  204.1 94.7 %reduce-scatter.3.cloned.1.call-done = f32[512,256]{0,1:T(8,128)} async-done(((f32[8192,256]{0,1:T(8,128)}), f32[512,256]{0,1:T(8,128)}) %reduce-scatter.3.cloned.1.call-update) | async-done | bytes 524304 | tf_op jit(solution)/shard_map/reduce_scatter | solution.py:54
  298.7 1.1 broadcast_multiply_fusion.1
  299.8 1.0 copy.11
  300.8 106.5 %reduce-scatter.5.cloned.1.call-done = f32[256,512]{1,0:T(8,128)} async-done(((f32[256,8192]{1,0:T(8,128)}), f32[256,512]{1,0:T(8,128)}) %reduce-scatter.5.cloned.1.call-update) | async-done | bytes 524304 | tf_op jit(solution)/shard_map/reduce_scatter | solution.py:52
  407.3 1.9 broadcast_multiply_fusion
  (7 shorter events, 0.0 us)
Async XLA Ops:
  7.2 56.3 %all-gather.3.cloned.1.call-start = ((), (), s32[]{:S(2)}) async-start(), calls=%async_computation.2 | async-start | bytes 4456448 | tf_op jit(solution)/shard_map/all_gather | solution.py:16
  7.9 109.4 %all-gather.5.cloned.1.call-start = ((), (), s32[]{:S(2)}) async-start(), calls=%async_computation.3 | async-start | bytes 4456448 | tf_op jit(solution)/shard_map/all_gather | solution.py:17
  8.6 290.1 %reduce-scatter.3.cloned.1.call-start = ((), (), s32[]{:S(2)}) async-start(), calls=%async_computation.4 | async-start | bytes 8912896 | tf_op jit(solution)/shard_map/reduce_scatter | solution.py:54
  196.7 210.6 %reduce-scatter.5.cloned.1.call-start = ((), (), s32[]{:S(2)}) async-start(), calls=%async_computation.5 | async-start | bytes 8912896 | tf_op jit(solution)/shard_map/reduce_scatter | solution.py:52
Sparse Core Ops, SparseCore 0:
  10.2 53.2 all-gather.2
  65.6 51.6 all-gather.4
  196.8 101.8 reduce-scatter.2
  302.7 104.5 reduce-scatter.4
where the time goes:
time: 416 us
  waiting for transfers between devices  304 us (73%)
  blocking collectives  58.9 us (14%)
  matrix products  31.7 us (8%)
  between operations  16.4 us (4%)
    reduce_scatter x1, waiting for transfers between devices, body(): lax.psum_scatter(up_term, 'dp', scatter_dimension=1, tiled=True) * scale  106 us
    reduce_scatter x1, waiting for transfers between devices, body(): lax.psum_scatter(lax.dot_general(tokens, latent_grad, (((0,), (0,)), ((),...  94.7 us
    psum x1, blocking collectives, body(): lax.psum((group_part, group_tally, depth_part, depth_tally), 'dp')  58.9 us
    all_gather x1, waiting for transfers between devices, body(): lax.all_gather(adapter_down, 'dp', axis=0, tiled=True)  52.1 us
    all_gather x1, waiting for transfers between devices, body(): lax.all_gather(adapter_up, 'dp', axis=1, tiled=True)  49.2 us
    dot_general x1, matrix products, body(): lax.dot_general(tokens, latent_grad, (((0,), (0,)), ((), ())), preferred_...  12.6 us
  transfers between devices with their start and end apart: 4, of which 4 were waited for; matrix products, arithmetic and copies ran while one was open for 3% of the time, Pallas kernels for 0%

commit v1 on v0

v1 whole, which is shorter than its diff:
```python
import functools

import jax
import jax.numpy as jnp
from jax import lax
from jax.experimental import pallas as pl
from jax.experimental.pallas import tpu as pltpu
from jax.sharding import PartitionSpec as P

MESH = pl.DeviceIdType.MESH
F32 = jnp.float32
BF16 = jnp.bfloat16
NT = (((1,), (1,)), ((), ()))
HALVES = 2


def chip_of(pos, n):
    if n != 8:
        return pos
    side = pos // 4
    return 2 * (pos + side * (7 - 2 * pos)) + side


def pos_of(chip, n):
    if n != 8:
        return chip
    side, height = chip % 2, chip // 2
    return height + side * (7 - 2 * height)


def kernel(
    n,
    tok, cho, down, up, lengths, parent, depth, reward,
    o_down, o_up, o_adv,
    X, C, S, Wd, Wu, lat_a, lat_b, q_a, ts, lg_a, lg_b, lhs_u, lhs_d, wcol, msg,
    st_u, rc_u, st_d, rc_d,
    s_x, s_w, s_xs, s_xr, s_ags, s_agr, s_pair_s, s_pair_r, s_ms, s_mr, s_rs, s_rr,
):
    T, R, bw = tok.shape[0], down.shape[1], down.shape[0]
    ndp = 2 * n
    me = lax.axis_index("dp")
    core, p = me % 2, pos_of(me // 2, n)
    sib = me + 1 - 2 * core
    hb, hs = n // 2, n // 2 - 1

    def at(k):
        return (p + k + 2 * n) % n

    def dev(pos, c):
        return 2 * chip_of(pos, n) + c

    def cols(pos, c):
        return pl.ds(pl.multiple_of(dev(pos, c) * bw, bw), bw)

    right, left = dev(at(1), core), dev(at(-1), core)
    mine = pl.ds(pl.multiple_of(core * T, T), T)

    def remote(src, dst, ss, rs, target):
        return pltpu.make_async_remote_copy(
            src_ref=src, dst_ref=dst, send_sem=ss, recv_sem=rs,
            device_id={"dp": target}, device_id_type=MESH,
        )

    w_local = [
        pltpu.make_async_copy(down, Wd.at[p], s_w.at[0]),
        pltpu.make_async_copy(up, Wu.at[p], s_w.at[1]),
    ]
    for cp in w_local:
        cp.start()

    barrier = pltpu.get_barrier_semaphore()

    @pl.loop(1, ndp)
    def _(o):
        pl.semaphore_signal(
            barrier, inc=1, device_id={"dp": (me + o) % ndp}, device_id_type=MESH
        )

    def x_local(k):
        pos = at(k)
        return [
            pltpu.make_async_copy(tok.at[:, cols(pos, core)], X.at[pos, mine], s_x.at[0, pos]),
            pltpu.make_async_copy(cho.at[:, cols(pos, core)], C.at[pos, mine], s_x.at[1, pos]),
        ]

    def x_pair(k):
        pos = at(k)
        return [
            remote(tok.at[:, cols(pos, 1 - core)], X.at[pos, mine], s_xs.at[0, pos], s_xr.at[0, pos], sib),
            remote(cho.at[:, cols(pos, 1 - core)], C.at[pos, mine], s_xs.at[1, pos], s_xr.at[1, pos], sib),
        ]

    order = [0]
    for s in range(1, hb + 1):
        order += [-s] if s == hb else [-s, s]
    for k in order:
        for cp in x_local(k):
            cp.start()
    pl.semaphore_wait(barrier, ndp - 1)

    hops = {0: (hb, hs), 1: (hs, hb)}

    def gather(arr, way, s):
        ref, own = ((Wd, down), (Wu, up))[arr]
        pos = at(-s if way == 0 else s)
        src = own if s == 0 else ref.at[pos]
        return remote(
            src, ref.at[pos], s_ags.at[arr, way, s], s_agr.at[arr, way, s], (right, left)[way]
        )

    def arrived(arr, way, s):
        ref = (Wd, Wu)[arr]
        pos = at(-(s + 1) if way == 0 else s + 1)
        return remote(
            ref.at[pos], ref.at[pos], s_ags.at[arr, way, s], s_agr.at[arr, way, s], (right, left)[way]
        )

    for arr in (0, 1):
        for way in (0, 1):
            gather(arr, way, 0).start()
    for k in order:
        for cp in x_pair(k):
            cp.start()

    lanes = 128

    def take_down(k, first=False):
        pos = at(k)
        x = X[pos]
        d = jnp.dot(x, Wd[pos], preferred_element_type=F32)
        lat_a[...] = d if first else lat_a[...] + d

    def take_up(k, first=False):
        pos = at(k)
        d = lax.dot_general(C[pos], Wu[pos], NT, preferred_element_type=F32)
        q_a[...] = d if first else q_a[...] + d

    def take_x(k, first=False):
        pos = at(k)
        t = jnp.zeros((2 * T, lanes), F32) if first else ts[...]
        for j in range(0, bw, lanes):
            sl = slice(j, j + lanes)
            t = t + X[pos, :, sl].astype(F32) * C[pos, :, sl].astype(F32)
        ts[...] = t

    def ready(k):
        for cp in x_local(k):
            cp.wait()
        for cp in x_pair(k):
            cp.wait_recv()

    for cp in w_local:
        cp.wait()
    ready(0)
    take_x(0, True)
    take_down(0, True)
    take_up(0, True)

    def pass_on(arr, s):
        got = []
        for way in (0, 1):
            if s - 1 < hops[arr][way]:
                arrived(arr, way, s - 1).wait_recv()
                if s < hops[arr][way]:
                    gather(arr, way, s).start()
                got.append(-s if way == 0 else s)
        return got

    pair_lat = remote(lat_a, lat_b, s_pair_s.at[0], s_pair_r.at[0], sib)
    for s in range(1, hb + 1):
        xs = [-s] if s == hb else [-s, s]
        for k in xs:
            ready(k)
            take_x(k)
        got = pass_on(0, s)
        for k in got:
            take_down(k)
        if s == hb:
            pair_lat.start()
        got = pass_on(1, s)
        for k in got:
            take_up(k)
    pair_lat.wait()
    lat = (lat_a[...] + lat_b[...]).astype(BF16).astype(F32)
    lhs_u[...] = lat.T.astype(BF16)

    prod = lat * q_a[...]
    t = ts[...]
    for j in range(0, R, lanes):
        t = t + prod[:, j : j + lanes]
    row = jnp.sum(t.T, axis=0, keepdims=True)
    msg[me, 0:1, :] = row[:, :T]
    msg[me, 1:2, :] = row[:, T:]
    ones = jnp.ones((1, T), F32)
    msg[me, 2:3, :] = ones * lengths[0].astype(F32)
    msg[me, 3:4, :] = ones * parent[0].astype(F32)
    msg[me, 4:5, :] = ones * depth[0].astype(F32)
    msg[me, 5:6, :] = ones * reward[0]
    msg[me, 6:8, :] = jnp.zeros((2, T), F32)

    def tell(o):
        return remote(msg.at[me], msg.at[me], s_ms.at[o], s_mr.at[me], (me + o) % ndp)

    def told(o):
        d = (me + o) % ndp
        return remote(msg.at[d], msg.at[d], s_ms.at[o], s_mr.at[d], d)

    @pl.loop(1, ndp)
    def _(o):
        tell(o).start()

    @pl.loop(1, ndp)
    def _(o):
        told(o).wait_recv()

    position = lax.broadcasted_iota(jnp.int32, (1, T), 1).astype(F32)
    base = me - core
    own = [msg[base], msg[base + 1]]
    zero = jnp.zeros((1, T), F32)
    sums = [[zero] * 4, [zero] * 4]
    for q in range(n):
        pair = [msg[2 * q], msg[2 * q + 1]]
        for c in (0, 1):
            score = pair[0][c : c + 1] + pair[1][c : c + 1]
            seg = pair[c]
            masked = jnp.where(position < seg[2:3], score, 0.0)
            for k in (0, 1):
                same_p = seg[3:4] == own[k][3:4]
                same_d = seg[4:5] == own[k][4:5]
                a = sums[k]
                sums[k] = [
                    a[0] + jnp.where(same_p, masked, 0.0),
                    a[1] + jnp.where(same_p, 1.0, 0.0),
                    a[2] + jnp.where(same_d, masked, 0.0),
                    a[3] + jnp.where(same_d, 1.0, 0.0),
                ]
    adv = []
    for k in (0, 1):
        score = own[0][k : k + 1] + own[1][k : k + 1]
        valid = position < own[k][2:3]
        masked = jnp.where(valid, score, 0.0)
        a = sums[k]
        val = (
            own[k][5:6] + masked
            - a[0] / jnp.maximum(a[1], 1.0)
            - 0.5 * (a[2] / jnp.maximum(a[3], 1.0))
        )
        adv.append(jnp.where(valid, val, 0.0))
    o_adv[...] = jnp.where(core == 0, adv[0], adv[1])
    weight = -jnp.concatenate(adv, axis=1)
    wcol[...] = jnp.broadcast_to(weight, (lanes, 2 * T)).T

    def slope(k):
        pos = at(k)
        for j in range(0, bw, lanes):
            sl = slice(j, j + lanes)
            S[pos, :, sl] = (wcol[...] * C[pos, :, sl].astype(F32)).astype(BF16)

    rows = R // HALVES
    rs_hops = {0: (hb, hs), 1: (hs, hb)}
    stage, landed = (st_u, st_d), (rc_u, rc_d)
    lhs, rhs = (lhs_u, lhs_d), (S, X)

    def partial(arr, pos, h):
        return jnp.dot(
            lhs[arr][h * rows : (h + 1) * rows, :], rhs[arr][pos], preferred_element_type=F32
        )

    def rs_copy(arr, way, s, h):
        slot = s if way == 0 else rs_hops[arr][0] + s
        part = pl.ds(h * rows, rows)
        return remote(
            stage[arr].at[slot, part], landed[arr].at[slot, part],
            s_rs.at[arr, slot, h], s_rr.at[arr, slot, h], (right, left)[way],
        )

    def rs_step(arr, s):
        for h in range(HALVES):
            part = slice(h * rows, (h + 1) * rows)
            for way in (0, 1):
                count = rs_hops[arr][way]
                if s >= count:
                    continue
                off = rs_hops[arr][0]
                slot = s if way == 0 else off + s
                pos = at(count - s if way == 0 else s - count)
                val = partial(arr, pos, h)
                if s > 0:
                    rs_copy(arr, way, s - 1, h).wait_recv()
                    val = val + landed[arr][slot - 1, part, :].astype(F32)
                stage[arr][slot, part, :] = val.astype(stage[arr].dtype)
                rs_copy(arr, way, s, h).start()

    def rs_end(arr):
        off = rs_hops[arr][0]
        for h in range(HALVES):
            part = slice(h * rows, (h + 1) * rows)
            val = partial(arr, p, h)
            for way in (1, 0) if rs_hops[arr][1] < off else (0, 1):
                last = rs_hops[arr][way] - 1
                rs_copy(arr, way, last, h).wait_recv()
                val = val + landed[arr][last if way == 0 else off + last, part, :].astype(F32)
            if arr == 0:
                o_up[part, :] = val
            else:
                o_down[:, part] = val.T

    slope(hb)
    slope(-hs)
    rs_step(0, 0)
    for k in range(-hs + 1, hb):
        slope(k)
    for k in range(n):
        d = lax.dot_general(S[k], Wu[k], NT, preferred_element_type=F32)
        lg_a[...] = d if k == 0 else lg_a[...] + d
    pair_lg = remote(lg_a, lg_b, s_pair_s.at[1], s_pair_r.at[1], sib)
    pair_lg.start()
    rs_step(0, 1)
    pair_lg.wait()
    lhs_d[...] = (lg_a[...] + lg_b[...]).T.astype(BF16)
    rs_step(1, 0)
    for s in range(2, hb):
        rs_step(0, s)
        rs_step(1, s - 1)
    rs_end(0)
    rs_step(1, hb - 1)
    rs_end(1)

    for k in order:
        for cp in x_pair(k):
            cp.wait_send()
    for arr in (0, 1):
        for way in (0, 1):
            for s in range(hops[arr][way]):
                gather(arr, way, s).wait_send()
            for s in range(rs_hops[arr][way]):
                for h in range(HALVES):
                    rs_copy(arr, way, s, h).wait_send()

    @pl.loop(1, ndp)
    def _(o):
        tell(o).wait_send()


def solution(mesh):
    ndp = mesh.shape["dp"]
    n = ndp // 2
    wire = BF16 if n <= 8 else F32

    def body(tokens, chosen_rows, adapter_down, adapter_up, lengths, parent, depth, reward):
        T, D = tokens.shape
        bw, R = adapter_down.shape
        hb = n // 2
        dma, vm = pltpu.SemaphoreType.DMA, pltpu.VMEM
        hbm = pl.BlockSpec(memory_space=pltpu.HBM)
        smem = pl.BlockSpec(memory_space=pltpu.SMEM)
        vmem = pl.BlockSpec(memory_space=pltpu.VMEM)
        g_down, g_up, adv = pl.pallas_call(
            functools.partial(kernel, n),
            out_shape=(
                jax.ShapeDtypeStruct((bw, R), F32),
                jax.ShapeDtypeStruct((R, bw), F32),
                jax.ShapeDtypeStruct((1, T), F32),
            ),
            in_specs=[hbm] * 4 + [smem] * 4,
            out_specs=(vmem,) * 3,
            scratch_shapes=[
                vm((n, 2 * T, bw), BF16),
                vm((n, 2 * T, bw), BF16),
                vm((n, 2 * T, bw), BF16),
                vm((n, bw, R), BF16),
                vm((n, R, bw), BF16),
                vm((2 * T, R), F32),
                vm((2 * T, R), F32),
                vm((2 * T, R), F32),
                vm((2 * T, 128), F32),
                vm((2 * T, R), F32),
                vm((2 * T, R), F32),
                vm((R, 2 * T), BF16),
                vm((R, 2 * T), BF16),
                vm((2 * T, 128), F32),
                vm((ndp, 8, T), F32),
                vm((n - 1, R, bw), wire),
                vm((n - 1, R, bw), wire),
                vm((n - 1, R, bw), wire),
                vm((n - 1, R, bw), wire),
                dma((2, n)),
                dma((2,)),
                dma((2, n)),
                dma((2, n)),
                dma((2, 2, hb)),
                dma((2, 2, hb)),
                dma((2,)),
                dma((2,)),
                dma((ndp,)),
                dma((ndp,)),
                dma((2, n - 1, HALVES)),
                dma((2, n - 1, HALVES)),
            ],
            compiler_params=pltpu.CompilerParams(
                collective_id=0, has_side_effects=True, vmem_limit_bytes=56 * 1024 * 1024
            ),
            cost_estimate=pl.CostEstimate(
                flops=10 * T * D * R, bytes_accessed=4 * T * D, transcendentals=0
            ),
        )(tokens, chosen_rows, adapter_down, adapter_up, lengths, parent, depth, reward)
        scale = 1.0 / jnp.sqrt(jnp.float32(T * ndp))
        return g_down * scale, g_up * scale, adv

    in_specs = (
        P(("groups", "dp"), None),
        P(("groups", "dp"), None),
        P("dp", None),
        P(None, "dp"),
        P(("groups", "dp")),
        P(("groups", "dp")),
        P(("groups", "dp")),
        P(("groups", "dp")),
    )
    out_specs = (P(("groups", "dp"), None), P("groups", "dp"), P(("groups", "dp"), None))
    return jax.shard_map(body, mesh=mesh, in_specs=in_specs, out_specs=out_specs, check_vma=False)
```

time: 416 us -> 109 us (0.26)
  waiting for transfers between devices: 304 us -> 0 us
  Pallas kernels: 0 us -> 100 us
  blocking collectives: 58.9 us -> 0 us
  matrix products: 31.7 us -> 0 us
  between operations: 16.4 us -> 3.22 us
    reduce_scatter x2 -> x0, waiting for transfers between devices: 201 us -> none  [the longest x1 106 us: body(): lax.psum_scatter(up_term, 'dp', scatter_dimension=1, tiled=True) * scale]
    all_gather x2 -> x0, waiting for transfers between devices: 101 us -> none  [the longest x1 52.1 us: body(): lax.all_gather(adapter_down, 'dp', axis=0, tiled=True)]
    pallas_call x0 -> x1, Pallas kernels: none -> 100 us  [body(): pl.pallas_call(functools.partial(kernel, n), out_shape=(jax.ShapeDtypeStr...]
    psum x1 -> x0, blocking collectives: 58.9 us -> none  [body(): lax.psum((group_part, group_tally, depth_part, depth_tally), 'dp')]
    dot_general x6 -> x0, matrix products: 31.7 us -> none  [the longest x1 12.6 us: body(): lax.dot_general(tokens, latent_grad, (((0,), (0,)), ((), ())), preferred_...]
  transfers between devices with their start and end apart: 4 -> 0, of which waited for: 4 -> 0; matrix products, arithmetic and copies ran while one was open for 3% -> 0% of each run, Pallas kernels for 0% -> 0%
where the time goes in v1:
time: 109 us; the launch traced here: 108 us
  Pallas kernels  100 us (92%)
  other arithmetic  3.75 us (3%)
  between operations  3.22 us (3%)
  local copies, waits for them, and re-layouts  1.24 us (1%)
    pallas_call x1, Pallas kernels, body(): pl.pallas_call(functools.partial(kernel, n), out_shape=(jax.ShapeDtypeStr...  100 us
    mul x2, other arithmetic, body(): return (g_down * scale, g_up * scale, adv)  3.75 us

profile of v1, /device:TPU:0, one launch (start us, length us, event | category | flops | bytes accessed | tf_op | source)
XLA Modules:
  0.0 108.4 jit_solution(17454691563023546502)
XLA Ops:
  3.2 100.2 %shard_map.103 = (f32[512,256]{1,0:T(8,128)}, f32[256,512]{1,0:T(8,128)}, f32[1,256]{1,0:T(1,128)}) custom-call(bf16[256,8192]{1,0:T(8,128)(2,1)} %tok.1, bf16[256,8192]{1,0:T(8,128)(2,1)} %cho.1, bf16[512,256]{1,0:T(8,128)(2,1)} %down.1, bf16[256,512]{1,0:T(8,128)(2,1)} %up.1, s32[1]{0:T(128)S(6)} %copy.12.lengths, s32[1]{0:T(128)S(6)} %copy.13.parent, ...), custom_call_target="tpu_custom_call" | custom-call | flops 5368709120 | bytes 8388608 | tf_op jit(solution)/shard_map/pallas_call | solution.py:358
  103.4 1.9 %broadcast_multiply_fusion.1 = f32[512,256]{1,0:T(8,128)} fusion(f32[512,256]{1,0:T(8,128)} %get-tuple-element.6), kind=kLoop, calls=%fused_computation.1 | loop fusion | flops 131072 | bytes 1048576 | tf_op jit(solution)/shard_map/mul | solution.py:408
  105.3 1.9 %broadcast_multiply_fusion = f32[256,512]{1,0:T(8,128)} fusion(f32[256,512]{1,0:T(8,128)} %get-tuple-element.7), kind=kLoop, calls=%fused_computation | loop fusion | flops 131072 | bytes 1048576 | tf_op jit(solution)/shard_map/mul | solution.py:408
  107.1 1.2 %copy.16 = f32[1,256]{1,0:T(1,128)} copy(f32[1,256]{1,0:T(1,128)} %get-tuple-element.14) | data formatting | bytes 2048

commit v2 on v1

--- a/solution.py
+++ b/solution.py
@@ -1,4 +1,5 @@
 import functools
+import math
 
 import jax
 import jax.numpy as jnp
@@ -29,12 +30,12 @@
 
 
 def kernel(
-    n,
+    n, scale,
     tok, cho, down, up, lengths, parent, depth, reward,
     o_down, o_up, o_adv,
     X, C, S, Wd, Wu, lat_a, lat_b, q_a, ts, lg_a, lg_b, lhs_u, lhs_d, wcol, msg,
     st_u, rc_u, st_d, rc_d,
-    s_x, s_w, s_xs, s_xr, s_ags, s_agr, s_pair_s, s_pair_r, s_ms, s_mr, s_rs, s_rr,
+    s_x, s_w, s_xs, s_xr, s_ags, s_agr, s_gs, s_gr, s_pair_s, s_pair_r, s_ms, s_mr, s_rs, s_rr,
 ):
     T, R, bw = tok.shape[0], down.shape[1], down.shape[0]
     ndp = 2 * n
@@ -42,6 +43,9 @@
     core, p = me % 2, pos_of(me // 2, n)
     sib = me + 1 - 2 * core
     hb, hs = n // 2, n // 2 - 1
+    group = lax.axis_index("groups")
+    odd = group % 2
+    other = group + 1 - 2 * odd
 
     def at(k):
         return (p + k + 2 * n) % n
@@ -76,6 +80,10 @@
             barrier, inc=1, device_id={"dp": (me + o) % ndp}, device_id_type=MESH
         )
 
+    pl.semaphore_signal(
+        barrier, inc=1, device_id={"groups": other}, device_id_type=MESH
+    )
+
     def x_local(k):
         pos = at(k)
         return [
@@ -96,23 +104,41 @@
     for k in order:
         for cp in x_local(k):
             cp.start()
-    pl.semaphore_wait(barrier, ndp - 1)
+    pl.semaphore_wait(barrier, ndp)
 
     hops = {0: (hb, hs), 1: (hs, hb)}
+
+    quarter = (bw // 4, R // 4)
+
+    def ringed(arr):
+        m = quarter[arr]
+        return pl.ds(pl.multiple_of(odd * m, m), 3 * m)
+
+    def across(arr, way, s, side):
+        ref, m = (Wd, Wu)[arr], quarter[arr]
+        pos = at(-(s + 1) if way == 0 else s + 1)
+        part = pl.ds(pl.multiple_of(side * 3 * m, m), m)
+        return pltpu.make_async_remote_copy(
+            src_ref=ref.at[pos, part], dst_ref=ref.at[pos, part],
+            send_sem=s_gs.at[arr, way, s], recv_sem=s_gr.at[arr, way, s],
+            device_id={"groups": other}, device_id_type=MESH,
+        )
 
     def gather(arr, way, s):
         ref, own = ((Wd, down), (Wu, up))[arr]
         pos = at(-s if way == 0 else s)
-        src = own if s == 0 else ref.at[pos]
+        part = ringed(arr)
+        src = own.at[part] if s == 0 else ref.at[pos, part]
         return remote(
-            src, ref.at[pos], s_ags.at[arr, way, s], s_agr.at[arr, way, s], (right, left)[way]
+            src, ref.at[pos, part], s_ags.at[arr, way, s], s_agr.at[arr, way, s], (right, left)[way]
         )
 
     def arrived(arr, way, s):
         ref = (Wd, Wu)[arr]
         pos = at(-(s + 1) if way == 0 else s + 1)
+        part = ringed(arr)
         return remote(
-            ref.at[pos], ref.at[pos], s_ags.at[arr, way, s], s_agr.at[arr, way, s], (right, left)[way]
+            ref.at[pos, part], ref.at[pos, part], s_ags.at[arr, way, s], s_agr.at[arr, way, s], (right, left)[way]
         )
 
     for arr in (0, 1):
@@ -157,14 +183,18 @@
     take_up(0, True)
 
     def pass_on(arr, s):
-        got = []
         for way in (0, 1):
             if s - 1 < hops[arr][way]:
                 arrived(arr, way, s - 1).wait_recv()
                 if s < hops[arr][way]:
                     gather(arr, way, s).start()
-                got.append(-s if way == 0 else s)
-        return got
+                across(arr, way, s - 1, odd).start()
+
+    def take(arr, s):
+        for way in (0, 1):
+            if s - 1 < hops[arr][way]:
+                across(arr, way, s - 1, 1 - odd).wait_recv()
+                (take_down, take_up)[arr](-s if way == 0 else s)
 
     pair_lat = remote(lat_a, lat_b, s_pair_s.at[0], s_pair_r.at[0], sib)
     for s in range(1, hb + 1):
@@ -172,14 +202,16 @@
         for k in xs:
             ready(k)
             take_x(k)
-        got = pass_on(0, s)
-        for k in got:
-            take_down(k)
+        pass_on(0, s)
+        if s > 1:
+            take(0, s - 1)
         if s == hb:
+            take(0, s)
             pair_lat.start()
-        got = pass_on(1, s)
-        for k in got:
-            take_up(k)
+        pass_on(1, s)
+        if s > 1:
+            take(1, s - 1)
+    take(1, hb)
     pair_lat.wait()
     lat = (lat_a[...] + lat_b[...]).astype(BF16).astype(F32)
     lhs_u[...] = lat.T.astype(BF16)
@@ -301,9 +333,9 @@
                 rs_copy(arr, way, last, h).wait_recv()
                 val = val + landed[arr][last if way == 0 else off + last, part, :].astype(F32)
             if arr == 0:
-                o_up[part, :] = val
+                o_up[part, :] = val * scale
             else:
-                o_down[:, part] = val.T
+                o_down[:, part] = (val * scale).T
 
     slope(hb)
     slope(-hs)
@@ -333,6 +365,7 @@
         for way in (0, 1):
             for s in range(hops[arr][way]):
                 gather(arr, way, s).wait_send()
+                across(arr, way, s, odd).wait_send()
             for s in range(rs_hops[arr][way]):
                 for h in range(HALVES):
                     rs_copy(arr, way, s, h).wait_send()
@@ -355,8 +388,9 @@
         hbm = pl.BlockSpec(memory_space=pltpu.HBM)
         smem = pl.BlockSpec(memory_space=pltpu.SMEM)
         vmem = pl.BlockSpec(memory_space=pltpu.VMEM)
-        g_down, g_up, adv = pl.pallas_call(
-            functools.partial(kernel, n),
+        scale = 1.0 / math.sqrt(T * ndp)
+        return pl.pallas_call(
+            functools.partial(kernel, n, scale),
             out_shape=(
                 jax.ShapeDtypeStruct((bw, R), F32),
                 jax.ShapeDtypeStruct((R, bw), F32),
@@ -390,6 +424,8 @@
                 dma((2, n)),
                 dma((2, 2, hb)),
                 dma((2, 2, hb)),
+                dma((2, 2, hb)),
+                dma((2, 2, hb)),
                 dma((2,)),
                 dma((2,)),
                 dma((ndp,)),
@@ -404,8 +440,6 @@
                 flops=10 * T * D * R, bytes_accessed=4 * T * D, transcendentals=0
             ),
         )(tokens, chosen_rows, adapter_down, adapter_up, lengths, parent, depth, reward)
-        scale = 1.0 / jnp.sqrt(jnp.float32(T * ndp))
-        return g_down * scale, g_up * scale, adv
 
     in_specs = (
         P(("groups", "dp"), None),

time: 109 us -> 104 us (0.954)
  Pallas kernels: 100 us -> 95.5 us
  other arithmetic: 3.75 us -> 0 us
  local copies, waits for them, and re-layouts: 1.24 us -> 4.98 us
    pallas_call x1, Pallas kernels: 100 us -> 95.5 us  [body(): pl.pallas_call(functools.partial(kernel, n, scale), out_shape=(jax.ShapeD...]
    mul x2 -> x0, other arithmetic: 3.75 us -> none  [body(): return (g_down * scale, g_up * scale, adv)]
    unnamed x1 -> x3, local copies, waits for them, and re-layouts: 1.24 us -> 4.98 us
where the time goes in v2:
time: 104 us
  Pallas kernels  95.5 us (92%)
  local copies, waits for them, and re-layouts  4.98 us (5%)
  between operations  3.22 us (3%)
    pallas_call x1, Pallas kernels, body(): pl.pallas_call(functools.partial(kernel, n, scale), out_shape=(jax.ShapeD...  95.5 us
    unnamed x3, local copies, waits for them, and re-layouts  4.98 us

profile of v2, /device:TPU:0, one launch (start us, length us, event | category | flops | bytes accessed | tf_op | source)
XLA Modules:
  0.0 103.7 jit_solution(1016582587035860200)
XLA Ops:
  3.2 95.5 %shard_map.103 = (f32[512,256]{1,0:T(8,128)}, f32[256,512]{1,0:T(8,128)}, f32[1,256]{1,0:T(1,128)}) custom-call(bf16[256,8192]{1,0:T(8,128)(2,1)} %tok.1, bf16[256,8192]{1,0:T(8,128)(2,1)} %cho.1, bf16[512,256]{1,0:T(8,128)(2,1)} %down.1, bf16[256,512]{1,0:T(8,128)(2,1)} %up.1, s32[1]{0:T(128)S(6)} %copy.14.lengths, s32[1]{0:T(128)S(6)} %copy.15.parent, ...), custom_call_target="tpu_custom_call" | custom-call | flops 5368709120 | bytes 8388608 | tf_op jit(solution)/shard_map/pallas_call | solution.py:392
  98.7 1.9 %copy.18 = f32[512,256]{1,0:T(8,128)} copy(f32[512,256]{1,0:T(8,128)} %get-tuple-element.6) | data formatting | bytes 1048576
  100.6 1.9 %copy.19 = f32[256,512]{1,0:T(8,128)} copy(f32[256,512]{1,0:T(8,128)} %get-tuple-element.7) | data formatting | bytes 1048576
  102.4 1.2 %copy.20 = f32[1,256]{1,0:T(1,128)} copy(f32[1,256]{1,0:T(1,128)} %get-tuple-element.8) | data formatting | bytes 2048

commit v3 on v2

--- a/solution.py
+++ b/solution.py
@@ -434,7 +434,7 @@
                 dma((2, n - 1, HALVES)),
             ],
             compiler_params=pltpu.CompilerParams(
-                collective_id=0, has_side_effects=True, vmem_limit_bytes=56 * 1024 * 1024
+                collective_id=0, has_side_effects=True, vmem_limit_bytes=44 * 1024 * 1024
             ),
             cost_estimate=pl.CostEstimate(
                 flops=10 * T * D * R, bytes_accessed=4 * T * D, transcendentals=0

time: 104 us -> 106 us (1.019)
  local copies, waits for them, and re-layouts: 4.98 us -> 8.42 us
  Pallas kernels: 95.5 us -> 94.2 us
    unnamed x3 -> x11, local copies, waits for them, and re-layouts: 4.98 us -> 8.42 us
    pallas_call x1, Pallas kernels: 95.5 us -> 94.2 us  [body(): pl.pallas_call(functools.partial(kernel, n, scale), out_shape=(jax.ShapeD...]
where the time goes in v3:
time: 106 us
  Pallas kernels  94.2 us (89%)
  local copies, waits for them, and re-layouts  8.42 us (8%)
  between operations  3.23 us (3%)
    pallas_call x1, Pallas kernels, body(): pl.pallas_call(functools.partial(kernel, n, scale), out_shape=(jax.ShapeD...  94.2 us
    unnamed x11, local copies, waits for them, and re-layouts  8.42 us

profile of v3, /device:TPU:0, one launch (start us, length us, event | category | flops | bytes accessed | tf_op | source)
XLA Modules:
  0.0 105.9 jit_solution(15575984548524293460)
XLA Ops:
  3.2 0.0 copy-start
  3.2 2.2 %copy-done = bf16[256,8192]{1,0:T(8,128)(2,1)S(1)} copy-done((bf16[256,8192]{1,0:T(8,128)(2,1)S(1)}, bf16[256,8192]{1,0:T(8,128)(2,1)}, u32[]{:S(2)}) %copy-start) | copy-done | bytes 4194328
  5.4 0.0 copy-start.1
  5.4 2.2 %copy-done.1 = bf16[256,8192]{1,0:T(8,128)(2,1)S(1)} copy-done((bf16[256,8192]{1,0:T(8,128)(2,1)S(1)}, bf16[256,8192]{1,0:T(8,128)(2,1)}, u32[]{:S(2)}) %copy-start.1) | copy-done | bytes 4194328
  7.6 0.0 copy-start.2
  7.6 0.9 copy-done.2
  8.5 0.0 copy-start.3
  8.5 0.9 copy-done.3
  9.5 94.2 %shard_map.103 = (f32[512,256]{1,0:T(8,128)S(1)}, f32[256,512]{1,0:T(8,128)S(1)}, f32[1,256]{1,0:T(1,128)S(1)}) custom-call(bf16[256,8192]{1,0:T(8,128)(2,1)S(1)} %copy-done, bf16[256,8192]{1,0:T(8,128)(2,1)S(1)} %copy-done.1, bf16[512,256]{1,0:T(8,128)(2,1)S(1)} %copy-done.2, bf16[256,512]{1,0:T(8,128)(2,1)S(1)} %copy-done.3, s32[1]{0:T(128)S(6)} %copy.14.lengths, ...), custom_call_target="tpu_custom_call" | custom-call | flops 5368709120 | bytes 8388608 | tf_op jit(solution)/shard_map/pallas_call | solution.py:392
  103.7 0.8 copy.18
  104.5 0.8 copy.19
  105.3 0.6 copy.20
Async XLA Ops:
  3.2 2.2 %copy-start = (bf16[256,8192]{1,0:T(8,128)(2,1)S(1)}, bf16[256,8192]{1,0:T(8,128)(2,1)}, u32[]{:S(2)}) copy-start(bf16[256,8192]{1,0:T(8,128)(2,1)} %tok.1) | copy-start | bytes 12582916
  5.4 2.2 %copy-start.1 = (bf16[256,8192]{1,0:T(8,128)(2,1)S(1)}, bf16[256,8192]{1,0:T(8,128)(2,1)}, u32[]{:S(2)}) copy-start(bf16[256,8192]{1,0:T(8,128)(2,1)} %cho.1) | copy-start | bytes 12582916
  7.6 0.9 copy-start.2
  8.5 0.9 copy-start.3
